TPU v7x, 512 devices: a whole 4x4x16 slice. The times are simulated.
512 devices in a mesh: row: 16 (over y, x), col: 32 (over z, core).
Axes of the slice: x: 4, y: 4, z: 16, core: 2. Of those that a mesh axis runs over, the one named last changes fastest.
Arguments:
- points: bfloat16 [262144, 256], P(('col', 'row')), may hold values from -6 to 6
- weights: bfloat16 [262144, 128], P(('col', 'row')), may hold values from -6 to 6
- near_blocks: int32 [2048, 16], P(('col', 'row')), may hold values from 0 to 2047, as said below
- proxies: bfloat16 [64, 256], replicated, may hold values from -6 to 6
Outputs:
- near_product: bfloat16 [262144, 128], P(('col', 'row'))
- factors: float32 [32768, 192], P(('col', 'row'))
Inputs may be any that keep to these rules, and one draw needn't show every extreme that they name: near_blocks[j, 0] = j; every entry of row j lies in the column group of j, that is in the same run of 64 blocks; entries may repeat.
All inputs are finite; a program needn't handle non-finite values.
Results may differ from a plain program's by a relative error of at most 0.01.
Values may be sent and summed in bfloat16 or wider, within the bound.
No kernel may reach another device: no remote copies, remote signals or barrier semaphores. Data moves between devices by JAX's collectives and lax.ppermute only.
A program may use at most 64 MiB of HBM per device.

v0:
```python
import jax
import jax.numpy as jnp
from jax import lax
from jax.sharding import PartitionSpec as P

DIM = 256
BLK = 128
NV = 128


def partner(value, axis, stride):
    mask = 2**stride
    pairs = [(source, source ^ mask) for source in range(lax.axis_size(axis))]
    return lax.ppermute(value, axis, pairs)


def kern_tile(left, right):
    cross = jnp.dot(left, right.T, preferred_element_type=jnp.float32)
    lnorm = jnp.sum(left.astype(jnp.float32) ** 2, axis=-1)
    rnorm = jnp.sum(right.astype(jnp.float32) ** 2, axis=-1)
    return jnp.exp(-(lnorm[:, None] + rnorm[None, :] - 2.0 * cross) * (2.0 / DIM))


def level_merge(lower_own, lower_other):
    high = lax.Precision.HIGHEST
    gram = jnp.dot(lower_own, lower_own.T, precision=high) + jnp.dot(
        lower_other, lower_other.T, precision=high
    )
    merged = jnp.linalg.cholesky(gram)
    transfer = lax.linalg.triangular_solve(merged, lower_own, left_side=True, lower=True).T
    return (merged, transfer)


def on_device(points, weights, near_blocks, proxies):
    n_local = near_blocks.shape[0]
    group_count = n_local * lax.axis_size("row")
    base = lax.axis_index("col") * group_count
    gathered = lax.all_gather(points, "row", axis=0, tiled=True)
    tblocks = gathered.reshape(group_count, BLK, DIM)
    local_ids = near_blocks - base
    sources = points.reshape(n_local, BLK, DIM)
    wblocks = weights.reshape(n_local, BLK, NV)
    targets = tblocks[local_ids]
    cross = jnp.einsum("jtad,jbd->jtab", targets, sources, preferred_element_type=jnp.float32)
    tnorm = jnp.sum(targets.astype(jnp.float32) ** 2, axis=-1)
    snorm = jnp.sum(sources.astype(jnp.float32) ** 2, axis=-1)
    dist = tnorm[:, :, :, None] + snorm[:, None, None, :] - 2.0 * cross
    tile = jnp.exp(-dist * (2.0 / DIM)).astype(jnp.bfloat16)
    contrib = jnp.einsum("jtab,jbv->jtav", tile, wblocks, preferred_element_type=jnp.float32)
    partial_value = jnp.zeros((group_count, BLK, NV), jnp.float32)
    partial_value = partial_value.at[local_ids.reshape(-1)].add(contrib.reshape(-1, BLK, NV))
    near_sum = lax.psum_scatter(
        partial_value.reshape(group_count * BLK, NV), "row", scatter_dimension=0, tiled=True
    )
    near_product = near_sum.astype(jnp.bfloat16)
    far = kern_tile(points, proxies)
    lower0 = jnp.linalg.cholesky(jnp.dot(far.T, far, precision=lax.Precision.HIGHEST))
    current = lower0
    transfers = []
    for level in range(2):
        sibling = partner(current, "col", level)
        current, transfer = level_merge(current, sibling)
        transfers.append(transfer)
    factors = jnp.concatenate([transfers[0], transfers[1], current.T], axis=1)
    return (near_product, factors)


def solution(mesh):
    placed = (P(("col", "row"), None), P(("col", "row"), None), P(("col", "row"), None), P())
    return jax.shard_map(
        on_device,
        mesh=mesh,
        in_specs=placed,
        out_specs=(P(("col", "row"), None), P(("col", "row"), None)),
        check_vma=False,
    )
```

profile of v0, /device:TPU:2, one launch (start us, length us, event | category | flops | bytes accessed | tf_op | source)
XLA Modules:
  0.0 213.1 jit_solution(5560618731934013219)
XLA Ops:
  7.2 0.0 copy-start
  7.2 0.0 all-gather.2.cloned.1.call-start
  7.2 0.7 all-gather.2.cloned.1.call-update
  7.9 0.0 reduce-scatter.2.cloned.1.call-start
  8.0 0.7 compare_select_fusion
  8.7 0.1 reshape.67
  8.7 0.1 reshape.77
  8.8 1.1 multiply_reduce_fusion.1
  9.9 72.4 %all-gather.2.cloned.1.call-done = bf16[8192,256]{1,0:T(8,128)(2,1)} async-done(((bf16[512,256]{1,0:T(8,128)(2,1)}), bf16[8192,256]{1,0:T(8,128)(2,1)}) %all-gather.2.cloned.1.call-update) | async-done | bytes 4194320 | tf_op jit(solution)/shard_map/all_gather | solution.py:38
  82.4 5.0 %gather_fusion = bf16[64,128,256]{2,1,0:T(8,128)(2,1)} fusion(bf16[64,128,256]{2,1,0:T(8,128)(2,1)} %bitcast.66, s32[1024]{0:T(1024)S(1)} %pad_clamp_fusion), kind=kCustom, calls=%fused_computation | custom fusion | bytes 8388864 | tf_op jit(solution)/shard_map/gather | solution.py:43
  87.3 0.0 copy-start.1
  87.3 3.4 %multiply_reduce_fusion = f32[4,16,128]{2,1,0:T(8,128)S(1)} fusion(bf16[4,16,128,256]{3,2,1,0:T(8,128)(2,1)} %bitcast.64), kind=kLoop, calls=%fused_computation.2 | loop fusion | flops 6283264 | bytes 4227072 | tf_op jit(solution)/shard_map/reduce_sum | solution.py:45
  90.7 0.0 copy-done
  90.7 0.0 copy-done.1
  90.7 4.9 %fusion = f32[4,16,128,128]{3,2,1,0:T(8,128)} fusion(bf16[4,128,128,1]{2,1,3,0:T(8,128)(2,1)S(1)} %bitcast.62, bf16[4,16,128,256]{3,2,1,0:T(8,128)(2,1)} %bitcast.65, bf16[4,128,256,1]{2,1,3,0:T(8,128)(2,1)S(1)} %bitcast.68, f32[4,128]{1,0:T(4,128)S(1)} %bitcast.69, f32[4,16,128]{2,1,0:T(8,128)S(1)} %multiply_reduce_fusion), kind=kOutput, calls=%fused_computation.4 | convolution fusion | flops 811597824 | bytes 8816640 | tf_op jit(solution)/shard_map/jtab,jbv->jtav/dot_general | solution.py:49
  95.6 2.5 %broadcast_in_dim.4 = f32[64,128,128]{2,1,0:T(8,128)} broadcast(f32[]{:T(128)} %constant.43.clone.1), dimensions={} | broadcast | bytes 4194308 | tf_op jit(solution)/shard_map/broadcast_in_dim | solution.py:50
  98.1 13.6 %scatter_fusion = f32[64,128,128]{2,1,0:T(8,128)} fusion(f32[64,128,128]{2,1,0:T(8,128)} %broadcast_in_dim.4, s32[64]{0:T(128)S(1)} %fusion.15, f32[64,128,128]{2,1,0:T(8,128)} %bitcast.67), kind=kCustom, calls=%fused_computation.1 | custom fusion | flops 1048576 | bytes 12583168 | tf_op jit(solution)/shard_map/scatter-add | solution.py:51
  111.8 0.0 copy-start.2
  111.8 0.0 reduce-scatter.2.cloned.1.call-update
  111.8 0.7 copy-done.2
  112.5 0.1 multiply_reduce_fusion.2
  112.6 0.2 fusion.4
  112.9 0.6 fusion.19
  113.5 0.1 copy.6
  113.6 5.8 %cholesky.59 = f32[64,64]{1,0:T(8,128)S(1)} custom-call(f32[64,64]{1,0:T(8,128)S(1)} %fusion.9), custom_call_target="Cholesky" | custom-call | tf_op jit(solution)/shard_map/jit(cholesky)/cholesky | solution.py:57
  119.5 0.6 compare_reduce_fusion.2
  120.1 0.7 fusion.10
  120.8 1.9 collective-permute-start
  122.7 0.2 fusion.20
  122.9 1.0 collective-permute-done
  123.9 0.2 convolution_add_fusion.1
  124.1 0.1 copy.9
  124.2 5.8 %cholesky.70 = f32[64,64]{1,0:T(8,128)S(1)} custom-call(f32[64,64]{1,0:T(8,128)S(1)} %fusion.8), custom_call_target="Cholesky" | custom-call | tf_op jit(solution)/shard_map/jit(cholesky)/cholesky | solution.py:29
  130.0 0.6 compare_reduce_fusion.1
  130.7 0.7 select_bitcast_fusion.1
  131.3 3.3 %collective-permute-start.1 = (f32[64,64]{1,0:T(8,128)S(1)}, f32[64,64]{1,0:T(8,128)S(1)}, u32[]{:S(2)}, u32[]{:S(2)}) collective-permute-start(f32[64,64]{1,0:T(8,128)S(1)} %get-tuple-element.7), channel_id=1, source_target_pairs={{0,2},{1,3},{2,0},{3,1},{4,6},{5,7},{6,4},{7,5},{8,10},{9,11},{10,... | collective-permute-start | bytes 49160 | tf_op jit(solution)/shard_map/ppermute | solution.py:14
  134.7 4.9 %custom-call.6 = f32[1,64,64]{1,2,0:T(8,128)S(1)} custom-call(f32[1,64,64]{2,1,0:T(8,128)S(1)} %get-tuple-element.6), custom_call_target="InvertDiagBlocksLowerTriangular" | custom-call | tf_op jit(solution)/shard_map/triangular_solve/custom-call.0 | solution.py:30
  139.6 0.2 fusion.21
  139.8 0.2 convolution_bitcast_fusion.1
  140.0 0.0 collective-permute-done.1
  140.0 0.2 convolution_add_fusion
  140.2 0.1 copy.13
  140.3 5.8 %cholesky.81 = f32[64,64]{1,0:T(8,128)S(1)} custom-call(f32[64,64]{1,0:T(8,128)S(1)} %fusion.6), custom_call_target="Cholesky" | custom-call | tf_op jit(solution)/shard_map/jit(cholesky)/cholesky | solution.py:29
  146.2 0.6 compare_reduce_fusion
  146.8 0.7 select_bitcast_fusion
  147.5 4.9 %custom-call.7 = f32[1,64,64]{1,2,0:T(8,128)S(1)} custom-call(f32[1,64,64]{2,1,0:T(8,128)S(1)} %get-tuple-element.10), custom_call_target="InvertDiagBlocksLowerTriangular" | custom-call | tf_op jit(solution)/shard_map/triangular_solve/custom-call.0 | solution.py:30
  152.4 0.3 convolution_bitcast_fusion
  152.7 0.7 copy.15
  153.4 51.3 %reduce-scatter.2.cloned.1.call-done = f32[512,128]{1,0:T(8,128)} async-done(((f32[8192,128]{1,0:T(8,128)}), f32[512,128]{1,0:T(8,128)}) %reduce-scatter.2.cloned.1.call-update) | async-done | bytes 262160 | tf_op jit(solution)/shard_map/reduce_scatter | solution.py:52
  204.7 1.6 convert_element_type.20
  (9 shorter events, 0.1 us)
Async XLA Ops:
  7.2 83.6 %copy-start = (bf16[512,128]{1,0:T(8,128)(2,1)S(1)}, bf16[512,128]{1,0:T(8,128)(2,1)}, u32[]{:S(2)}) copy-start(bf16[512,128]{1,0:T(8,128)(2,1)} %param.8) | copy-start | bytes 393220
  7.2 75.2 %all-gather.2.cloned.1.call-start = ((), (), s32[]{:S(2)}) async-start(), calls=%async_computation.1 | async-start | bytes 4456448 | tf_op jit(solution)/shard_map/all_gather | solution.py:38
  7.9 196.8 %reduce-scatter.2.cloned.1.call-start = ((), (), s32[]{:S(2)}) async-start(), calls=%async_computation.2 | async-start | bytes 4456448 | tf_op jit(solution)/shard_map/reduce_scatter | solution.py:52
  87.3 3.4 %copy-start.1 = (bf16[512,256]{1,0:T(8,128)(2,1)S(1)}, bf16[512,256]{1,0:T(8,128)(2,1)}, u32[]{:S(2)}) copy-start(bf16[512,256]{1,0:T(8,128)(2,1)} %param.7) | copy-start | bytes 786436
  111.8 0.8 copy-start.2
  120.8 3.1 %collective-permute-start = (f32[64,64]{1,0:T(8,128)S(1)}, f32[64,64]{1,0:T(8,128)S(1)}, u32[]{:S(2)}, u32[]{:S(2)}) collective-permute-start(f32[64,64]{1,0:T(8,128)S(1)} %fusion.10), channel_id=1, source_target_pairs={{0,1},{1,0},{2,3},{3,2},{4,5},{5,4},{6,7},{7,6},{8,9},{9,8},{10,11... | collective-permute-start | bytes 49160 | tf_op jit(solution)/shard_map/ppermute | solution.py:14
  131.3 8.7 %collective-permute-start.1 = (f32[64,64]{1,0:T(8,128)S(1)}, f32[64,64]{1,0:T(8,128)S(1)}, u32[]{:S(2)}, u32[]{:S(2)}) collective-permute-start(f32[64,64]{1,0:T(8,128)S(1)} %get-tuple-element.7), channel_id=1, source_target_pairs={{0,2},{1,3},{2,0},{3,1},{4,6},{5,7},{6,4},{7,5},{8,10},{9,11},{10,... | collective-permute-start | bytes 49160 | tf_op jit(solution)/shard_map/ppermute | solution.py:14
Sparse Core Ops, SparseCore 0:
  11.0 71.2 all-gather.1
  111.9 92.7 reduce-scatter.1
where the time goes:
time: 214 us; the launch traced here: 213 us
  waiting for transfers between devices  125 us (58%)
  other arithmetic  51.9 us (24%)
  between operations  14.3 us (7%)
  local copies, waits for them, and re-layouts  9.3 us (4%)
  matrix products  6.97 us (3%)
  starting transfers between devices  5.31 us (2%)
    all_gather x1, waiting for transfers between devices, on_device(): gathered = lax.all_gather(points, 'row', axis=0, tiled=True)  72.4 us
    reduce_scatter x1, waiting for transfers between devices, on_device(): lax.psum_scatter(partial_value.reshape(group_count * BLK, NV), 'row', sca...  51.3 us
    scatter-add x1, other arithmetic, on_device(): partial_value.at[local_ids.reshape(-1)].add(contrib.reshape(-1, BLK, NV))  13.6 us
    another operation x6, other arithmetic, level_merge(): merged = jnp.linalg.cholesky(gram)  13 us
    another operation x4, other arithmetic, level_merge(): lax.linalg.triangular_solve(merged, lower_own, left_side=True, lower=True)  11.1 us
    another operation x3, other arithmetic, on_device(): jnp.linalg.cholesky(jnp.dot(far.T, far, precision=lax.Precision.HIGHEST))  6.52 us
    ppermute x2, starting transfers between devices, partner(): return lax.ppermute(value, axis, pairs)  5.24 us
    gather x1, local copies, waits for them, and re-layouts, on_device(): targets = tblocks[local_ids]  4.97 us
  transfers between devices with their start and end apart: 4, of which 3 were waited for; matrix products, arithmetic and copies ran while one was open for 17% of the time, Pallas kernels for 0%

commit v1 on v0

--- a/solution.py
+++ b/solution.py
@@ -6,6 +6,11 @@
 DIM = 256
 BLK = 128
 NV = 128
+
+
+def swapped_in(x, name, dim):
+    sent = jnp.stack([x] * lax.axis_size(name))
+    return jnp.concatenate(lax.all_to_all(sent, name, 0, 0), axis=dim)
 
 
 def partner(value, axis, stride):
@@ -35,7 +40,7 @@
     n_local = near_blocks.shape[0]
     group_count = n_local * lax.axis_size("row")
     base = lax.axis_index("col") * group_count
-    gathered = lax.all_gather(points, "row", axis=0, tiled=True)
+    gathered = swapped_in(points, "row", 0)
     tblocks = gathered.reshape(group_count, BLK, DIM)
     local_ids = near_blocks - base
     sources = points.reshape(n_local, BLK, DIM)

time: 214 us -> 214 us (level)
  waiting for transfers between devices: 125 us -> 109 us
  starting transfers between devices: 5.31 us -> 21 us
  local copies, waits for them, and re-layouts: 9.3 us -> 12.7 us
    all_gather x1 -> x0, waiting for transfers between devices: 72.4 us -> none  [on_device(): gathered = lax.all_gather(points, 'row', axis=0, tiled=True)]
    all_to_all x0 -> x1, waiting for transfers between devices: none -> 50.9 us  [swapped_in(): return jnp.concatenate(lax.all_to_all(sent, name, 0, 0), axis=dim)]
    all_to_all x0 -> x1, starting transfers between devices: none -> 10.3 us  [swapped_in(): return jnp.concatenate(lax.all_to_all(sent, name, 0, 0), axis=dim)]
    reduce_scatter x1, waiting for transfers between devices: 51.3 us -> 56.8 us  [on_device(): lax.psum_scatter(partial_value.reshape(group_count * BLK, NV), 'row', sca...]
    ppermute x2, starting transfers between devices: 5.24 us -> 10.7 us  [partner(): return lax.ppermute(value, axis, pairs)]
    another operation x0 -> x1, local copies, waits for them, and re-layouts: none -> 3.36 us  [swapped_in(): sent = jnp.stack([x] * lax.axis_size(name))]
  transfers between devices with their start and end apart: 4 -> 4, of which waited for: 3 -> 3; matrix products, arithmetic and copies ran while one was open for 17% -> 16% of each run, Pallas kernels for 0% -> 0%
where the time goes in v1:
time: 214 us
  waiting for transfers between devices  109 us (51%)
  other arithmetic  50.2 us (23%)
  starting transfers between devices  21 us (10%)
  between operations  14.3 us (7%)
  local copies, waits for them, and re-layouts  12.7 us (6%)
  matrix products  6.97 us (3%)
    reduce_scatter x1, waiting for transfers between devices, on_device(): lax.psum_scatter(partial_value.reshape(group_count * BLK, NV), 'row', sca...  56.8 us
    all_to_all x1, waiting for transfers between devices, swapped_in(): return jnp.concatenate(lax.all_to_all(sent, name, 0, 0), axis=dim)  50.9 us
    scatter-add x1, other arithmetic, on_device(): partial_value.at[local_ids.reshape(-1)].add(contrib.reshape(-1, BLK, NV))  13.6 us
    another operation x6, other arithmetic, level_merge(): merged = jnp.linalg.cholesky(gram)  13 us
    another operation x4, other arithmetic, level_merge(): lax.linalg.triangular_solve(merged, lower_own, left_side=True, lower=True)  11.1 us
    ppermute x2, starting transfers between devices, partner(): return lax.ppermute(value, axis, pairs)  10.7 us
    all_to_all x1, starting transfers between devices, swapped_in(): return jnp.concatenate(lax.all_to_all(sent, name, 0, 0), axis=dim)  10.3 us
    another operation x3, other arithmetic, on_device(): jnp.linalg.cholesky(jnp.dot(far.T, far, precision=lax.Precision.HIGHEST))  6.52 us
  transfers between devices with their start and end apart: 4, of which 3 were waited for; matrix products, arithmetic and copies ran while one was open for 16% of the time, Pallas kernels for 0%

profile of v1, /device:TPU:2, one launch (start us, length us, event | category | flops | bytes accessed | tf_op | source)
XLA Modules:
  0.0 213.8 jit_solution(10297023917232793025)
XLA Ops:
  7.2 0.0 copy-start
  7.2 3.4 %stack.2 = bf16[16,512,256]{2,1,0:T(8,128)(2,1)} broadcast(bf16[512,256]{1,0:T(8,128)(2,1)} %param.7), dimensions={1,2} | broadcast | bytes 4456448 | tf_op jit(solution)/shard_map/stack | solution.py:12
  10.5 0.0 copy-start.3
  10.5 0.0 copy-start.1
  10.5 10.3 %all-to-all-start = ((bf16[16,512,256]{2,1,0:T(8,128)(2,1)}), bf16[16,512,256]{2,1,0:T(8,128)(2,1)}, u32[]{:S(2)}, u32[]{:S(2)}) async-start(bf16[16,512,256]{2,1,0:T(8,128)(2,1)} %stack.2), calls=%async_computation | async-start | bytes 8388608 | tf_op jit(solution)/shard_map/all_to_all | solution.py:13
  20.8 0.0 reduce-scatter.2.cloned.1.call-start
  20.9 0.0 copy-done.3
  20.9 0.1 reshape.66
  21.0 0.1 reshape.75
  21.1 0.0 copy-done.1
  21.1 0.2 multiply_reduce_fusion.1
  21.3 50.9 %all-to-all-done = bf16[16,512,256]{2,1,0:T(8,128)(2,1)} async-done(((bf16[16,512,256]{2,1,0:T(8,128)(2,1)}), bf16[16,512,256]{2,1,0:T(8,128)(2,1)}, u32[]{:S(2)}, u32[]{:S(2)}) %all-to-all-start) | async-done | bytes 4194336 | tf_op jit(solution)/shard_map/all_to_all | solution.py:13
  72.2 5.0 %gather_fusion = bf16[64,128,256]{2,1,0:T(8,128)(2,1)} fusion(bf16[64,128,256]{2,1,0:T(8,128)(2,1)} %bitcast.1, s32[1024]{0:T(1024)S(1)} %pad_clamp_fusion), kind=kCustom, calls=%fused_computation | custom fusion | bytes 8388864 | tf_op jit(solution)/shard_map/gather | solution.py:48
  77.2 3.3 %multiply_reduce_fusion = f32[4,16,128]{2,1,0:T(8,128)S(1)} fusion(bf16[4,16,128,256]{3,2,1,0:T(8,128)(2,1)} %bitcast.64), kind=kLoop, calls=%fused_computation.2 | loop fusion | flops 6283264 | bytes 4227072 | tf_op jit(solution)/shard_map/reduce_sum | solution.py:50
  80.5 0.0 copy-done
  80.5 4.9 %fusion = f32[4,16,128,128]{3,2,1,0:T(8,128)} fusion(bf16[4,128,128,1]{2,1,3,0:T(8,128)(2,1)S(1)} %bitcast.62, bf16[4,16,128,256]{3,2,1,0:T(8,128)(2,1)} %bitcast.65, bf16[4,128,256,1]{2,1,3,0:T(8,128)(2,1)S(1)} %bitcast.67, f32[4,128]{1,0:T(4,128)S(1)} %bitcast.68, f32[4,16,128]{2,1,0:T(8,128)S(1)} %multiply_reduce_fusion), kind=kOutput, calls=%fused_computation.4 | convolution fusion | flops 811597824 | bytes 8816640 | tf_op jit(solution)/shard_map/jtab,jbv->jtav/dot_general | solution.py:54
  85.4 2.5 %broadcast_in_dim.4 = f32[64,128,128]{2,1,0:T(8,128)} broadcast(f32[]{:T(128)} %constant.43.clone.1), dimensions={} | broadcast | bytes 4194308 | tf_op jit(solution)/shard_map/broadcast_in_dim | solution.py:55
  87.9 13.6 %scatter_fusion = f32[64,128,128]{2,1,0:T(8,128)} fusion(f32[64,128,128]{2,1,0:T(8,128)} %broadcast_in_dim.4, s32[64]{0:T(128)S(1)} %fusion.15, f32[64,128,128]{2,1,0:T(8,128)} %bitcast.66), kind=kCustom, calls=%fused_computation.1 | custom fusion | flops 1048576 | bytes 12583168 | tf_op jit(solution)/shard_map/scatter-add | solution.py:56
  101.6 0.0 copy-start.2
  101.6 0.0 reduce-scatter.2.cloned.1.call-update
  101.6 0.7 copy-done.2
  102.3 0.1 multiply_reduce_fusion.2
  102.4 0.2 fusion.4
  102.7 0.6 fusion.19
  103.3 0.1 copy.16
  103.4 5.8 %cholesky.59 = f32[64,64]{1,0:T(8,128)S(1)} custom-call(f32[64,64]{1,0:T(8,128)S(1)} %fusion.9), custom_call_target="Cholesky" | custom-call | tf_op jit(solution)/shard_map/jit(cholesky)/cholesky | solution.py:62
  109.2 0.6 compare_reduce_fusion.2
  109.9 0.7 fusion.10
  110.5 1.9 collective-permute-start
  112.5 0.2 fusion.20
  112.7 1.0 collective-permute-done
  113.6 0.2 convolution_add_fusion.1
  113.8 0.1 copy.19
  113.9 5.8 %cholesky.70 = f32[64,64]{1,0:T(8,128)S(1)} custom-call(f32[64,64]{1,0:T(8,128)S(1)} %fusion.8), custom_call_target="Cholesky" | custom-call | tf_op jit(solution)/shard_map/jit(cholesky)/cholesky | solution.py:34
  119.8 0.6 compare_reduce_fusion.1
  120.5 0.7 select_bitcast_fusion.1
  121.1 8.7 %collective-permute-start.1 = (f32[64,64]{1,0:T(8,128)S(1)}, f32[64,64]{1,0:T(8,128)S(1)}, u32[]{:S(2)}, u32[]{:S(2)}) collective-permute-start(f32[64,64]{1,0:T(8,128)S(1)} %get-tuple-element.9), channel_id=1, source_target_pairs={{0,2},{1,3},{2,0},{3,1},{4,6},{5,7},{6,4},{7,5},{8,10},{9,11},{10,... | collective-permute-start | bytes 49160 | tf_op jit(solution)/shard_map/ppermute | solution.py:19
  129.9 4.9 %custom-call.6 = f32[1,64,64]{1,2,0:T(8,128)S(1)} custom-call(f32[1,64,64]{2,1,0:T(8,128)S(1)} %get-tuple-element.8), custom_call_target="InvertDiagBlocksLowerTriangular" | custom-call | tf_op jit(solution)/shard_map/triangular_solve/custom-call.0 | solution.py:35
  134.8 0.2 fusion.21
  135.0 0.2 convolution_bitcast_fusion.1
  135.2 0.0 collective-permute-done.1
  135.2 0.2 convolution_add_fusion
  135.4 0.1 copy.23
  135.5 5.8 %cholesky.81 = f32[64,64]{1,0:T(8,128)S(1)} custom-call(f32[64,64]{1,0:T(8,128)S(1)} %fusion.6), custom_call_target="Cholesky" | custom-call | tf_op jit(solution)/shard_map/jit(cholesky)/cholesky | solution.py:34
  141.4 0.6 compare_reduce_fusion
  142.0 0.7 select_bitcast_fusion
  142.7 4.9 %custom-call.7 = f32[1,64,64]{1,2,0:T(8,128)S(1)} custom-call(f32[1,64,64]{2,1,0:T(8,128)S(1)} %get-tuple-element.12), custom_call_target="InvertDiagBlocksLowerTriangular" | custom-call | tf_op jit(solution)/shard_map/triangular_solve/custom-call.0 | solution.py:35
  147.6 0.3 convolution_bitcast_fusion
  147.9 0.7 copy.25
  148.6 56.8 %reduce-scatter.2.cloned.1.call-done = f32[512,128]{1,0:T(8,128)} async-done(((f32[8192,128]{1,0:T(8,128)}), f32[512,128]{1,0:T(8,128)}) %reduce-scatter.2.cloned.1.call-update) | async-done | bytes 262160 | tf_op jit(solution)/shard_map/reduce_scatter | solution.py:57
  205.4 1.6 convert_element_type.20
  (10 shorter events, 0.1 us)
Async XLA Ops:
  7.2 73.4 %copy-start = (bf16[512,128]{1,0:T(8,128)(2,1)S(1)}, bf16[512,128]{1,0:T(8,128)(2,1)}, u32[]{:S(2)}) copy-start(bf16[512,128]{1,0:T(8,128)(2,1)} %param.8) | copy-start | bytes 393220
  10.5 10.4 %copy-start.3 = (s32[4,16]{1,0:T(4,128)S(1)}, s32[4,16]{1,0:T(4,128)}, u32[]{:S(2)}) copy-start(s32[4,16]{1,0:T(4,128)} %param.9) | copy-start | bytes 772
  10.5 10.5 %copy-start.1 = (bf16[512,256]{1,0:T(8,128)(2,1)S(1)}, bf16[512,256]{1,0:T(8,128)(2,1)}, u32[]{:S(2)}) copy-start(bf16[512,256]{1,0:T(8,128)(2,1)} %param.7) | copy-start | bytes 786436
  10.5 61.7 %all-to-all-start = ((bf16[16,512,256]{2,1,0:T(8,128)(2,1)}), bf16[16,512,256]{2,1,0:T(8,128)(2,1)}, u32[]{:S(2)}, u32[]{:S(2)}) async-start(bf16[16,512,256]{2,1,0:T(8,128)(2,1)} %stack.2), calls=%async_computation | async-start | bytes 8388608 | tf_op jit(solution)/shard_map/all_to_all | solution.py:13
  20.8 184.5 %reduce-scatter.2.cloned.1.call-start = ((), (), s32[]{:S(2)}) async-start(), calls=%async_computation.2 | async-start | bytes 4456448 | tf_op jit(solution)/shard_map/reduce_scatter | solution.py:57
  101.6 0.8 copy-start.2
  110.5 3.1 %collective-permute-start = (f32[64,64]{1,0:T(8,128)S(1)}, f32[64,64]{1,0:T(8,128)S(1)}, u32[]{:S(2)}, u32[]{:S(2)}) collective-permute-start(f32[64,64]{1,0:T(8,128)S(1)} %fusion.10), channel_id=1, source_target_pairs={{0,1},{1,0},{2,3},{3,2},{4,5},{5,4},{6,7},{7,6},{8,9},{9,8},{10,11... | collective-permute-start | bytes 49160 | tf_op jit(solution)/shard_map/ppermute | solution.py:19
  121.1 14.1 %collective-permute-start.1 = (f32[64,64]{1,0:T(8,128)S(1)}, f32[64,64]{1,0:T(8,128)S(1)}, u32[]{:S(2)}, u32[]{:S(2)}) collective-permute-start(f32[64,64]{1,0:T(8,128)S(1)} %get-tuple-element.9), channel_id=1, source_target_pairs={{0,2},{1,3},{2,0},{3,1},{4,6},{5,7},{6,4},{7,5},{8,10},{9,11},{10,... | collective-permute-start | bytes 49160 | tf_op jit(solution)/shard_map/ppermute | solution.py:19
Sparse Core Ops, SparseCore 0:
  101.7 103.6 reduce-scatter.1
